TPU v7x, 32 devices: a whole 2x2x4 slice. The times are simulated.
32 devices in a mesh: parts: 2 (over y), latent: 4 (over z), tok: 2 (over x), sub: 2 (over core).
Axes of the slice: x: 2, y: 2, z: 4, core: 2. Of those that a mesh axis runs over, the one named last changes fastest.
Arguments:
- resid: bfloat16 [64, 3584], P(('parts', 'latent', 'tok'), 'sub'), parts along dimension 0, may hold values from -6 to 6
- enc_weight: bfloat16 [3584, 65536], P('sub', ('latent', 'tok')), may hold values from -0.09375 to 0.09375
- enc_bias: float32 [65536], P(('latent', 'tok')), may hold values from -3 to 3
- dec_weight: bfloat16 [65536, 3584], P(('latent', 'tok'), 'sub'), may hold values from -0.0625 to 0.0625
- dec_bias: float32 [3584], P('sub'), may hold values from -3 to 3
- spans: int32 [16, 32], P('parts'), parts along dimension 0, may hold values from 0 to 1, as said below
- owners: int32 [16], P('parts'), parts along dimension 0, may hold values from 0 to 1, as said below
Outputs:
- recon: bfloat16 [64, 3584], P(('parts', 'latent', 'tok'), 'sub'), parts along dimension 0
- owned: bfloat16 [24, 65536], P(('parts', 'tok'), 'latent'), parts along dimension 0
There are 2 independent parts, one for each index of `parts`. A program takes and returns all parts, laid end to end along the dimension named above; an argument that names none is the same for every part. Nothing has to cross between parts.
Inputs may be any that keep to these rules, and one draw needn't show every extreme that they name: `spans`: each column holds exactly one 1; each document's ones form one contiguous run of at least one row, documents in order. `owners`: no owner holds more than 6 documents, and one owner holds exactly 6.
All inputs are finite; a program needn't handle non-finite values.
Results may differ from a plain program's by a relative error of at most 0.0055.
Values may be sent and summed in bfloat16 or wider, within the bound.
A program may use at most 128 MiB of HBM per device.

v0:
```python
import jax
import jax.numpy as jnp
from jax import lax
from jax.sharding import PartitionSpec as P

CAP = 6


def per_device(resid, enc_weight, enc_bias, dec_weight, dec_bias, spans, owners):
    centered = (resid.astype(jnp.float32) - dec_bias).astype(jnp.bfloat16)
    partial_pre = jnp.dot(
        lax.all_gather(centered, ("latent", "tok"), axis=0, tiled=True),
        enc_weight,
        preferred_element_type=jnp.float32,
    )
    summed_pre = lax.psum(partial_pre, "sub")
    acts = jnp.maximum(summed_pre + enc_bias, 0.0).astype(jnp.bfloat16)
    summed = lax.psum_scatter(
        jnp.dot(acts, dec_weight, preferred_element_type=jnp.float32),
        ("latent", "tok"),
        scatter_dimension=0,
        tiled=True,
    )
    recon = (summed + dec_bias).astype(jnp.bfloat16)
    counts = jnp.sum(spans, axis=1).astype(jnp.float32)
    pooled = (
        jnp.dot(spans.astype(jnp.bfloat16), acts, preferred_element_type=jnp.float32)
        / counts[:, None]
    ).astype(jnp.bfloat16)
    owner_count = lax.axis_size("tok")
    hits = (owners[:, None] == jnp.arange(owner_count, dtype=jnp.int32)[None, :]).astype(jnp.int32)
    before = jnp.cumsum(hits, axis=0) - hits
    slots = jnp.sum(before * hits, axis=1)
    target = owners * CAP + slots
    select = (target[None, :] == jnp.arange(owner_count * CAP, dtype=jnp.int32)[:, None]).astype(
        jnp.bfloat16
    )
    outgoing = jnp.dot(select, pooled, preferred_element_type=jnp.float32).astype(jnp.bfloat16)
    owned = lax.all_to_all(outgoing, "tok", split_axis=0, concat_axis=1, tiled=True)
    return (recon, owned)


def solution(mesh):
    placed = (
        P(("parts", "latent", "tok"), "sub"),
        P("sub", ("latent", "tok")),
        P(("latent", "tok")),
        P(("latent", "tok"), "sub"),
        P("sub"),
        P("parts", None),
        P("parts"),
    )
    return jax.shard_map(
        per_device,
        mesh=mesh,
        in_specs=placed,
        out_specs=(P(("parts", "latent", "tok"), "sub"), P(("parts", "tok"), "latent")),
        check_vma=False,
    )
```

profile of v0, /device:TPU:0, one launch (start us, length us, event | category | flops | bytes accessed | tf_op | source)
XLA Modules:
  0.0 170.5 jit_solution(6532914947817027076)
XLA Ops:
  7.2 0.0 copy-start.4
  7.2 0.0 copy-start.3
  7.2 0.0 copy-start.1
  7.2 0.0 all-reduce.4.cloned.1.call-start
  7.2 0.7 fusion.4
  8.0 32.4 %all-gather = bf16[8,4,1792]{2,1,0:T(4,128)(2,1)S(1)} all-gather(bf16[1,4,1792]{2,1,0:T(4,128)(2,1)S(1)} %fusion.4), channel_id=1, replica_groups=mesh['parts'=2,'latent'=4,'tok'=2,'sub'=2] {'latent','tok'}, dimensions={0}, use_global_device_ids=true | all-gather | bytes 129024 | tf_op jit(solution)/shard_map/all_gather | solution.py:12
  40.4 13.1 %fusion.12 = f32[32,8192]{1,0:T(8,128)} fusion(bf16[32,1792]{1,0:T(8,128)(2,1)S(1)} %reshape.15, bf16[1792,8192]{1,0:T(8,128)(2,1)} %param.8), kind=kOutput, calls=%fused_computation.19 | convolution fusion | flops 939524096 | bytes 30523392 | tf_op jit(solution)/shard_map/dot_general | solution.py:11
  53.5 0.0 copy-start.5
  53.5 0.0 copy-start.2
  53.5 0.0 all-reduce.4.cloned.1.call-update
  53.5 0.0 all-reduce.6.cloned.1.call-start
  53.5 0.0 copy-done.4
  53.6 0.2 reduce_window_sum.11
  53.8 0.0 copy-done.3
  53.8 0.1 reduce_sum.19
  53.9 20.2 %all-reduce.4.cloned.1.call-done = f32[32,8192]{1,0:T(8,128)} async-done(((f32[32,8192]{1,0:T(8,128)}), f32[32,8192]{1,0:T(8,128)}) %all-reduce.4.cloned.1.call-update) | async-done | bytes 1048592 | tf_op jit(solution)/shard_map/psum | solution.py:16
  74.1 0.0 copy-done.1
  74.1 0.0 copy-start
  74.1 15.5 %fusion.2 = f32[32,1792]{1,0:T(8,128)} fusion(bf16[8192,1792]{1,0:T(8,128)(2,1)} %param.10, f32[32,8192]{1,0:T(8,128)} %all-reduce.4.cloned.1.call-done, f32[8192]{0:T(1024)S(1)} %copy-done.1), kind=kOutput, calls=%fused_computation.5 | convolution fusion | flops 940310528 | bytes 30670848 | tf_op jit(solution)/shard_map/dot_general | solution.py:19
  89.7 0.0 all-reduce.6.cloned.1.call-update
  89.7 0.0 copy-done
  89.7 0.3 convolution_convert_fusion
  90.0 0.8 all_to_all.14
  90.8 3.4 %all-to-all-start = ((bf16[2,6,8192]{2,1,0:T(8,128)(2,1)}), bf16[2,6,8192]{2,1,0:T(8,128)(2,1)S(1)}, u32[]{:S(2)}, u32[]{:S(2)}) async-start(bf16[2,6,8192]{2,1,0:T(8,128)(2,1)} %all_to_all.14), calls=%async_computation | async-start | bytes 524288 | tf_op jit(solution)/shard_map/all_to_all | solution.py:39
  94.3 0.0 copy-done.5
  94.3 0.6 dynamic-slice
  95.5 5.5 %all-to-all-done = bf16[2,6,8192]{2,1,0:T(8,128)(2,1)S(1)} async-done(((bf16[2,6,8192]{2,1,0:T(8,128)(2,1)}), bf16[2,6,8192]{2,1,0:T(8,128)(2,1)S(1)}, u32[]{:S(2)}, u32[]{:S(2)}) %all-to-all-start) | async-done | bytes 196640 | tf_op jit(solution)/shard_map/all_to_all | solution.py:39
  101.0 60.5 %all-reduce.6.cloned.1.call-done = f32[32,1792]{1,0:T(8,128)} async-done(((f32[32,1792]{1,0:T(8,128)}), f32[32,1792]{1,0:T(8,128)}) %all-reduce.6.cloned.1.call-update) | async-done | bytes 229392
  161.5 0.0 copy-done.2
  161.5 1.4 fusion.3
  162.9 0.7 copy.12
  (5 shorter events, 0.1 us)
Async XLA Ops:
  7.2 46.4 %copy-start.4 = (s32[8]{0:T(128)S(1)}, s32[8]{0:T(128)}, u32[]{:S(2)}) copy-start(s32[8]{0:T(128)} %param.13) | copy-start | bytes 100
  7.2 46.6 %copy-start.3 = (s32[8,32]{1,0:T(8,128)S(1)}, s32[8,32]{1,0:T(8,128)}, u32[]{:S(2)}) copy-start(s32[8,32]{1,0:T(8,128)} %param.12) | copy-start | bytes 3076
  7.2 67.0 %copy-start.1 = (f32[8192]{0:T(1024)S(1)}, f32[8192]{0:T(1024)}, u32[]{:S(2)}) copy-start(f32[8192]{0:T(1024)} %param.9) | copy-start | bytes 98308
  7.2 66.9 %all-reduce.4.cloned.1.call-start = ((), (), s32[]{:S(2)}) async-start(), calls=%async_computation.1 | async-start | bytes 2097152 | tf_op jit(solution)/shard_map/psum | solution.py:16
  53.5 40.8 %copy-start.5 = (u32[32]{0:T(128)S(1)}, u32[32]{0:T(128)}, u32[]{:S(2)}) copy-start(u32[32]{0:T(128)} %constant.13) | copy-start | bytes 388
  53.5 108.0 %copy-start.2 = (f32[1792]{0:T(1024)S(1)}, f32[1792]{0:T(1024)}, u32[]{:S(2)}) copy-start(f32[1792]{0:T(1024)} %param.11) | copy-start | bytes 21508
  53.5 108.0 %all-reduce.6.cloned.1.call-start = ((), (), s32[]{:S(2)}) async-start(), calls=%async_computation.2 | async-start | bytes 458752
  74.1 15.5 %copy-start = (f32[32,8192]{1,0:T(8,128)S(1)}, f32[32,8192]{1,0:T(8,128)}, u32[]{:S(2)}) copy-start(f32[32,8192]{1,0:T(8,128)} %all-reduce.4.cloned.1.call-done) | copy-start | bytes 3145732
  90.8 10.2 %all-to-all-start = ((bf16[2,6,8192]{2,1,0:T(8,128)(2,1)}), bf16[2,6,8192]{2,1,0:T(8,128)(2,1)S(1)}, u32[]{:S(2)}, u32[]{:S(2)}) async-start(bf16[2,6,8192]{2,1,0:T(8,128)(2,1)} %all_to_all.14), calls=%async_computation | async-start | bytes 524288 | tf_op jit(solution)/shard_map/all_to_all | solution.py:39
Sparse Core Ops, SparseCore 0:
  53.6 20.4 all-reduce.3
  89.8 71.6 all-reduce.5
where the time goes:
time: 171 us; the launch traced here: 170 us
  waiting for transfers between devices  86.3 us (50%)
  blocking collectives  32.4 us (19%)
  matrix products  28.9 us (17%)
  between operations  14.8 us (9%)
  starting transfers between devices  3.52 us (2%)
  other arithmetic  2.49 us (1%)
  local copies, waits for them, and re-layouts  2.12 us (1%)
    unnamed x3, waiting for transfers between devices  60.5 us
    all_gather x1, blocking collectives, per_device(): lax.all_gather(centered, ('latent', 'tok'), axis=0, tiled=True)  32.4 us
    psum x1, waiting for transfers between devices, per_device(): summed_pre = lax.psum(partial_pre, 'sub')  20.2 us
    dot_general x1, matrix products, per_device(): jnp.dot(acts, dec_weight, preferred_element_type=jnp.float32)  15.5 us
    dot_general x1, matrix products, per_device(): jnp.dot(lax.all_gather(centered, ('latent', 'tok'), axis=0, tiled=True),...  13.1 us
    all_to_all x1, waiting for transfers between devices, per_device(): lax.all_to_all(outgoing, 'tok', split_axis=0, concat_axis=1, tiled=True)  5.51 us
    all_to_all x1, starting transfers between devices, per_device(): lax.all_to_all(outgoing, 'tok', split_axis=0, concat_axis=1, tiled=True)  3.44 us
  transfers between devices with their start and end apart: 3, of which 3 were waited for; matrix products, arithmetic and copies ran while one was open for 1% of the time, Pallas kernels for 0%

commit v1 on v0

v1 whole, which is shorter than its diff:
```python
import functools

import jax
import jax.numpy as jnp
from jax import lax
from jax.experimental import pallas as pl
from jax.experimental.pallas import tpu as pltpu
from jax.sharding import PartitionSpec as P

CAP = 6
PAD = 8
MESH = pl.DeviceIdType.MESH
BF16 = jnp.bfloat16
F32 = jnp.float32


def chunked(total, step):
    return [(at, min(step, total - at)) for at in range(0, total, step)]


def kernel(
    sizes, enc_parts, dec_parts,
    resid, enc_hbm, enc_bias, dec_hbm, dec_bias, spans, owners,
    recon, owned,
    wenc, wdec, xg, xf, x2, mg, pe, pr, acts,
    ysend, yown, yrecv, bsend, bown, brecv, csend, cown, crecv, psend, precv,
    wenc_sem, wdec_sem, gz_sem, gy_sem, gx_sem, m_sem, e_sem, a_sem, b_sem, c_sem, p_sem,
):
    n_p, n_l, n_t = sizes
    p, l, t, s = (lax.axis_index(name) for name in ("parts", "latent", "tok", "sub"))
    rows = resid.shape[0]
    half = acts.shape[1]
    total_rows = n_p * n_l * n_t * rows
    part_rows = n_l * n_t * rows

    def at(dp=0, dl=0, dt=0, ds=0):
        return (
            lax.rem(p + dp, n_p), lax.rem(l + dl, n_l), lax.rem(t + dt, n_t), lax.rem(s + ds, 2)
        )

    sent = []

    def send(src, dst, sems, index, device):
        copy = pltpu.make_async_remote_copy(
            src_ref=src, dst_ref=dst, send_sem=sems.at[(0,) + index],
            recv_sem=sems.at[(1,) + index], device_id=device, device_id_type=MESH,
        )
        copy.start()
        sent.append(copy)
        return copy

    base = pl.multiple_of(p * half, half)
    enc_copies = []
    for j, (start, width) in enumerate(enc_parts):
        copy = pltpu.make_async_copy(
            enc_hbm.at[:, pl.ds(pl.multiple_of(base + start, 128), width)],
            wenc.at[:, pl.ds(start, width)], wenc_sem.at[j],
        )
        copy.start()
        enc_copies.append(copy)

    barrier = pltpu.get_barrier_semaphore()
    peers = [at(ds=1)]
    peers += [at(dl=k) for k in range(1, n_l)]
    peers += [at(dp=a, dt=b) for a in range(n_p) for b in range(n_t) if a or b]
    for peer in peers:
        pl.semaphore_signal(barrier, inc=1, device_id=peer, device_id_type=MESH)

    xg[t, p, l] = (resid[...].astype(F32) - dec_bias[...]).astype(BF16)

    docs = spans.shape[0]
    row_i = lax.broadcasted_iota(jnp.int32, (docs, docs), 0)
    col_i = lax.broadcasted_iota(jnp.int32, (docs, docs), 1)
    across = jnp.broadcast_to(owners[...], (docs, docs))
    down = jnp.sum(jnp.where(row_i == col_i, across, 0), axis=1, keepdims=True)
    same = jnp.where((down == across) & (row_i < col_i), 1, 0)
    slots = jnp.sum(same, axis=0, keepdims=True)
    target = owners[...] * PAD + slots
    select = target == lax.broadcasted_iota(jnp.int32, (n_t * PAD, docs), 0)
    member = jnp.dot(
        jnp.where(select, 1.0, 0.0).astype(BF16), spans[...].astype(F32).astype(BF16),
        preferred_element_type=F32,
    )
    place = lax.broadcasted_iota(jnp.int32, (part_rows, total_rows), 1)
    source = lax.broadcasted_iota(jnp.int32, (part_rows, total_rows), 0)
    r_at = lax.rem(place, rows)
    l_at = lax.rem(lax.div(place, rows), n_l)
    p_at = lax.rem(lax.div(place, rows * n_l), n_p)
    t_at = lax.div(place, rows * n_l * n_p)
    wanted = jnp.where(p_at == p, (l_at * n_t + t_at) * rows + r_at, -1)
    mg[p] = jnp.dot(
        member.astype(BF16), jnp.where(source == wanted, 1.0, 0.0).astype(BF16),
        preferred_element_type=F32,
    )

    pl.semaphore_wait(barrier, len(peers))

    copies = [
        send(xg.at[t, p, l], xg.at[t, p, l], gz_sem, (k - 1,), at(dl=k)) for k in range(1, n_l)
    ]
    m_copies = [send(mg.at[p], mg.at[p], m_sem, (k - 1,), at(dp=k)) for k in range(1, n_p)]
    dec_copies = []
    for j, (start, width) in enumerate(dec_parts):
        copy = pltpu.make_async_copy(
            dec_hbm.at[pl.ds(base, half), pl.ds(start, width)],
            wdec.at[:, pl.ds(start, width)], wdec_sem.at[j],
        )
        copy.start()
        dec_copies.append(copy)
    for copy in copies:
        copy.wait_recv()
    y_copies = [send(xg.at[t, p], xg.at[t, p], gy_sem, (k - 1,), at(dp=k)) for k in range(1, n_p)]
    x_copies = [
        send(xg.at[t, p], xg.at[t, p], gx_sem, (0, k - 1), at(dt=k)) for k in range(1, n_t)
    ]
    for m, copy in enumerate(y_copies, 1):
        copy.wait_recv()
        came = lax.rem(p + n_p - m, n_p)
        x_copies += [
            send(xg.at[t, came], xg.at[t, came], gx_sem, (m, k - 1), at(dt=k))
            for k in range(1, n_t)
        ]
    for copy in x_copies:
        copy.wait_recv()
    block = 0
    for a in range(n_t):
        for b in range(n_p):
            for c in range(n_l):
                xf[pl.ds(block * rows, rows), :] = xg[a, b, c].astype(F32)
                block += 1
    x2[...] = xf[...].astype(BF16)

    e_copies = []
    for j, (start, width) in enumerate(enc_parts):
        cols = pl.ds(start, width)
        enc_copies[j].wait()
        pe[:, cols] = jnp.dot(x2[...], wenc[:, cols], preferred_element_type=F32)
        e_copies.append(send(pe.at[:, cols], pr.at[:, cols], e_sem, (j,), at(ds=1)))

    def make_acts(j):
        start, width = enc_parts[j]
        cols = pl.ds(start, width)
        e_copies[j].wait_recv()
        bias = enc_bias[:, pl.ds(pl.multiple_of(base + start, 128), width)]
        acts[:, cols] = jnp.maximum(pe[:, cols] + pr[:, cols] + bias, 0.0).astype(BF16)

    a_copies, b_copies, c_copies = {}, {}, {}

    def decode(c):
        start, width = dec_parts[c]
        cols = pl.ds(start, width)
        dec_copies[c].wait()
        if c == 0:
            y = None
            for j, (k0, kw) in enumerate(enc_parts):
                make_acts(j)
                term = jnp.dot(
                    acts[:, pl.ds(k0, kw)], wdec[pl.ds(k0, kw), cols], preferred_element_type=F32
                )
                y = term if y is None else y + term
        else:
            y = jnp.dot(acts[...], wdec[:, cols], preferred_element_type=F32)
        tall = total_rows // n_t
        for a in range(n_t):
            piece = y[a * tall:(a + 1) * tall]
            ysend[a, :, cols] = piece.astype(BF16)
            yown[a, :, cols] = piece
        a_copies[c] = []
        for k in range(1, n_t):
            peer = at(dt=k)
            a_copies[c].append(
                send(ysend.at[peer[2], :, cols], yrecv.at[k - 1, :, cols], a_sem, (c, k - 1), peer)
            )

    def sum_x(c):
        start, width = dec_parts[c]
        cols = pl.ds(start, width)
        total = yown[t, :, cols]
        for k, copy in enumerate(a_copies[c]):
            copy.wait_recv()
            total += yrecv[k, :, cols].astype(F32)
        tall = total_rows // (n_t * n_p)
        for a in range(n_p):
            piece = total[a * tall:(a + 1) * tall]
            bsend[a, :, cols] = piece.astype(BF16)
            bown[a, :, cols] = piece
        b_copies[c] = []
        for k in range(1, n_p):
            peer = at(dp=k)
            b_copies[c].append(
                send(bsend.at[peer[0], :, cols], brecv.at[k - 1, :, cols], b_sem, (c, k - 1), peer)
            )

    def sum_y(c):
        start, width = dec_parts[c]
        cols = pl.ds(start, width)
        total = bown[p, :, cols]
        for k, copy in enumerate(b_copies[c]):
            copy.wait_recv()
            total += brecv[k, :, cols].astype(F32)
        for a in range(n_l):
            piece = total[a * rows:(a + 1) * rows]
            csend[a, :, cols] = piece.astype(BF16)
            cown[a, :, cols] = piece
        c_copies[c] = []
        for k in range(1, n_l):
            peer = at(dl=k)
            c_copies[c].append(
                send(csend.at[peer[1], :, cols], crecv.at[k - 1, :, cols], c_sem, (c, k - 1), peer)
            )

    def sum_z(c):
        start, width = dec_parts[c]
        cols = pl.ds(start, width)
        total = cown[l, :, cols]
        for k, copy in enumerate(c_copies[c]):
            copy.wait_recv()
            total += crecv[k, :, cols].astype(F32)
        recon[:, cols] = (total + dec_bias[:, cols]).astype(BF16)

    def pool():
        for copy in m_copies:
            copy.wait_recv()
        spread = jnp.concatenate([mg[a] for a in range(n_p)], axis=0)
        counts = jnp.maximum(jnp.sum(spread, axis=1, keepdims=True), 1.0)
        pooled = jnp.dot(spread.astype(BF16), acts[...], preferred_element_type=F32) / counts
        for a in range(n_p * n_t):
            psend[a] = pooled[a * PAD:a * PAD + CAP].astype(BF16)
        mine = p * n_t + t
        precv[mine] = psend[mine]
        copies = []
        for a in range(n_p):
            for b in range(n_t):
                if a or b:
                    peer = at(dp=a, dt=b)
                    copies.append(
                        send(psend.at[peer[0] * n_t + peer[2]], precv.at[mine], p_sem, (a, b), peer)
                    )
        return copies

    steps = len(dec_parts)
    pool_copies = []
    for c in range(steps + 3):
        if c < steps:
            decode(c)
        if c == 0:
            pool_copies = pool()
        if 0 <= c - 1 < steps:
            sum_x(c - 1)
        if 0 <= c - 2 < steps:
            sum_y(c - 2)
        if c == steps:
            for copy in pool_copies:
                copy.wait_recv()
            for a in range(n_p):
                for b in range(n_t):
                    owned[:, pl.ds((b * n_p + a) * half, half)] = precv[a * n_t + b]
        if 0 <= c - 3 < steps:
            sum_z(c - 3)
    for copy in sent:
        copy.wait_send()


def per_device(sizes, resid, enc_weight, enc_bias, dec_weight, dec_bias, spans, owners):
    n_p, n_l, n_t = sizes
    rows, width = resid.shape
    half = enc_weight.shape[1] // n_p
    total = rows * n_p * n_l * n_t
    enc_parts = chunked(half, 1024)
    dec_parts = chunked(width, 512)
    vmem = pl.BlockSpec(memory_space=pltpu.VMEM)
    hbm = pl.BlockSpec(memory_space=pl.ANY)
    dma = pltpu.SemaphoreType.DMA
    x_rows, y_rows = total // n_t, total // (n_t * n_p)
    more = lambda n: max(n - 1, 1)
    steps = len(dec_parts)
    return pl.pallas_call(
        functools.partial(kernel, sizes, enc_parts, dec_parts),
        out_shape=(
            jax.ShapeDtypeStruct((rows, width), BF16),
            jax.ShapeDtypeStruct((CAP, half * n_p * n_t), BF16),
        ),
        in_specs=[vmem, hbm, vmem, hbm, vmem, vmem, vmem],
        out_specs=(vmem, vmem),
        scratch_shapes=[
            pltpu.VMEM((width, half), BF16),
            pltpu.VMEM((half, width), BF16),
            pltpu.VMEM((n_t, n_p, n_l, rows, width), BF16),
            pltpu.VMEM((total, width), F32),
            pltpu.VMEM((total, width), BF16),
            pltpu.VMEM((n_p, n_t * PAD, total), F32),
            pltpu.VMEM((total, half), F32),
            pltpu.VMEM((total, half), F32),
            pltpu.VMEM((total, half), BF16),
            pltpu.VMEM((n_t, x_rows, width), BF16),
            pltpu.VMEM((n_t, x_rows, width), F32),
            pltpu.VMEM((more(n_t), x_rows, width), BF16),
            pltpu.VMEM((n_p, y_rows, width), BF16),
            pltpu.VMEM((n_p, y_rows, width), F32),
            pltpu.VMEM((more(n_p), y_rows, width), BF16),
            pltpu.VMEM((n_l, rows, width), BF16),
            pltpu.VMEM((n_l, rows, width), F32),
            pltpu.VMEM((more(n_l), rows, width), BF16),
            pltpu.VMEM((n_p * n_t, CAP, half), BF16),
            pltpu.VMEM((n_p * n_t, CAP, half), BF16),
            dma((len(enc_parts),)),
            dma((steps,)),
            dma((2, more(n_l))),
            dma((2, more(n_p))),
            dma((2, n_p, more(n_t))),
            dma((2, more(n_p))),
            dma((2, len(enc_parts))),
            dma((2, steps, more(n_t))),
            dma((2, steps, more(n_p))),
            dma((2, steps, more(n_l))),
            dma((2, n_p, n_t)),
        ],
        compiler_params=pltpu.CompilerParams(
            collective_id=0, has_side_effects=True, vmem_limit_bytes=58 * 1024 * 1024
        ),
        cost_estimate=pl.CostEstimate(
            flops=4 * total * width * half, bytes_accessed=4 * width * half, transcendentals=0
        ),
    )(
        resid, enc_weight, enc_bias[None, :], dec_weight, dec_bias[None, :], spans, owners[None, :]
    )


def solution(mesh):
    placed = (
        P(("parts", "latent", "tok"), "sub"),
        P("sub", ("latent", "tok")),
        P(("latent", "tok")),
        P(("latent", "tok"), "sub"),
        P("sub"),
        P("parts", None),
        P("parts"),
    )
    sizes = tuple(mesh.shape[name] for name in ("parts", "latent", "tok"))
    return jax.shard_map(
        functools.partial(per_device, sizes),
        mesh=mesh,
        in_specs=placed,
        out_specs=(P(("parts", "latent", "tok"), "sub"), P(("parts", "tok"), "latent")),
        check_vma=False,
    )
```

time: 171 us -> 44.5 us (0.26)
  waiting for transfers between devices: 86.3 us -> 0 us
  Pallas kernels: 0 us -> 39.3 us
  blocking collectives: 32.4 us -> 0 us
  matrix products: 28.9 us -> 0 us
  between operations: 14.8 us -> 0.64 us
  starting transfers between devices: 3.52 us -> 0 us
  other arithmetic: 2.49 us -> 0 us
  local copies, waits for them, and re-layouts: 2.12 us -> 4.28 us
    unnamed x3 -> x0, waiting for transfers between devices: 60.5 us -> none
    pallas_call x0 -> x1, Pallas kernels: none -> 39.3 us  [per_device(): pl.pallas_call(functools.partial(kernel, sizes, enc_parts, dec_parts), ou...]
    all_gather x1 -> x0, blocking collectives: 32.4 us -> none  [per_device(): lax.all_gather(centered, ('latent', 'tok'), axis=0, tiled=True)]
    dot_general x3 -> x0, matrix products: 28.9 us -> none  [the longest x1 15.5 us: per_device(): jnp.dot(acts, dec_weight, preferred_element_type=jnp.float32)]
    psum x1 -> x0, waiting for transfers between devices: 20.2 us -> none  [per_device(): summed_pre = lax.psum(partial_pre, 'sub')]
    all_to_all x1 -> x0, waiting for transfers between devices: 5.51 us -> none  [per_device(): lax.all_to_all(outgoing, 'tok', split_axis=0, concat_axis=1, tiled=True)]
    all_to_all x1 -> x0, starting transfers between devices: 3.44 us -> none  [per_device(): lax.all_to_all(outgoing, 'tok', split_axis=0, concat_axis=1, tiled=True)]
  transfers between devices with their start and end apart: 3 -> 0, of which waited for: 3 -> 0; matrix products, arithmetic and copies ran while one was open for 1% -> 0% of each run, Pallas kernels for 0% -> 0%
where the time goes in v1:
time: 44.5 us; the launch traced here: 44.2 us
  Pallas kernels  39.3 us (88%)
  local copies, waits for them, and re-layouts  4.28 us (10%)
  between operations  0.64 us (1%)
    pallas_call x1, Pallas kernels, per_device(): pl.pallas_call(functools.partial(kernel, sizes, enc_parts, dec_parts), ou...  39.3 us
    unnamed x2, local copies, waits for them, and re-layouts  2.99 us
    broadcast_in_dim x1, local copies, waits for them, and re-layouts, per_device(): dec_bias[None, :]  1.3 us

profile of v1, /device:TPU:0, one launch (start us, length us, event | category | flops | bytes accessed | tf_op | source)
XLA Modules:
  0.0 44.2 jit_solution(13922663944673856566)
XLA Ops:
  0.6 1.3 %broadcast_in_dim.10.dec_bias = f32[1,1792]{1,0:T(1,128)} reshape(f32[1792]{0:T(1024)} %param.11) | data formatting | bytes 14336 | tf_op jit(solution)/shard_map/broadcast_in_dim | solution.py:325
  1.9 39.3 %shard_map.86 = (bf16[4,1792]{1,0:T(4,128)(2,1)}, bf16[6,16384]{1,0:T(8,128)(2,1)}) custom-call(bf16[4,1792]{1,0:T(4,128)(2,1)} %resid.1, bf16[1792,8192]{1,0:T(8,128)(2,1)} %enc_hbm.1, f32[1,8192]{1,0:T(1,128)} %bitcast.2, bf16[8192,1792]{1,0:T(8,128)(2,1)} %dec_hbm.1, f32[1,1792]{1,0:T(1,128)} %broadcast_in_dim.10.dec_bias, s32[8,32]{1,0:T(8,128)} %spans.1, ...), custom_call_target="tpu_custom_call" | custom-call | flops 1879048192 | bytes 29360128 | tf_op jit(solution)/shard_map/pallas_call | solution.py:277
  41.2 1.3 %copy.11 = bf16[4,1792]{1,0:T(4,128)(2,1)} copy(bf16[4,1792]{1,0:T(4,128)(2,1)} %get-tuple-element.4) | data formatting | bytes 28672
  42.5 1.7 %copy.12 = bf16[6,16384]{1,0:T(8,128)(2,1)} copy(bf16[6,16384]{1,0:T(8,128)(2,1)} %get-tuple-element.5) | data formatting | bytes 393216

commit v2 on v1

--- a/solution.py
+++ b/solution.py
@@ -20,11 +20,11 @@
 
 def kernel(
     sizes, enc_parts, dec_parts,
-    resid, enc_hbm, enc_bias, dec_hbm, dec_bias, spans, owners,
-    recon, owned,
-    wenc, wdec, xg, xf, x2, mg, pe, pr, acts,
-    ysend, yown, yrecv, bsend, bown, brecv, csend, cown, crecv, psend, precv,
-    wenc_sem, wdec_sem, gz_sem, gy_sem, gx_sem, m_sem, e_sem, a_sem, b_sem, c_sem, p_sem,
+    resid_hbm, enc_hbm, enc_bias_hbm, dec_hbm, dec_bias_hbm, spans_hbm, owners_hbm,
+    recon_hbm, owned_hbm,
+    resid, enc_bias, dec_bias_flat, dec_bias, spans, owners, recon, wenc, wdec, xg, xf, x2, mg, pe, pr, acts,
+    ysend, yown, yrecv, csend, cown, crecv, psend, precv,
+    small_sem, out_sem, wenc_sem, wdec_sem, gz_sem, g_sem, m_sem, e_sem, a_sem, c_sem, p_sem,
 ):
     n_p, n_l, n_t = sizes
     p, l, t, s = (lax.axis_index(name) for name in ("parts", "latent", "tok", "sub"))
@@ -50,13 +50,26 @@
         return copy
 
     base = pl.multiple_of(p * half, half)
+    small = [
+        pltpu.make_async_copy(src, dst, small_sem.at[j])
+        for j, (src, dst) in enumerate((
+            (resid_hbm, resid),
+            (dec_bias_hbm, dec_bias_flat),
+            (spans_hbm, spans),
+            (owners_hbm, owners),
+            (enc_bias_hbm.at[:, pl.ds(base, half)], enc_bias),
+        ))
+    ]
+    for copy in small:
+        copy.start()
+
     enc_copies = []
     for j, (start, width) in enumerate(enc_parts):
         copy = pltpu.make_async_copy(
             enc_hbm.at[:, pl.ds(pl.multiple_of(base + start, 128), width)],
             wenc.at[:, pl.ds(start, width)], wenc_sem.at[j],
         )
-        copy.start()
+        copy.start(priority=1)
         enc_copies.append(copy)
 
     barrier = pltpu.get_barrier_semaphore()
@@ -65,6 +78,10 @@
     peers += [at(dp=a, dt=b) for a in range(n_p) for b in range(n_t) if a or b]
     for peer in peers:
         pl.semaphore_signal(barrier, inc=1, device_id=peer, device_id_type=MESH)
+
+    for copy in small:
+        copy.wait()
+    dec_bias[...] = dec_bias_flat[...].reshape(dec_bias.shape)
 
     xg[t, p, l] = (resid[...].astype(F32) - dec_bias[...]).astype(BF16)
 
@@ -95,9 +112,16 @@
 
     pl.semaphore_wait(barrier, len(peers))
 
-    copies = [
+    others = [(a, b) for a in range(n_p) for b in range(n_t) if a or b]
+
+    def spread_rows(k, came):
+        ref = xg.at[t, p, came]
+        return [send(ref, ref, g_sem, (k, a, b), at(dp=a, dt=b)) for a, b in others]
+
+    z_copies = [
         send(xg.at[t, p, l], xg.at[t, p, l], gz_sem, (k - 1,), at(dl=k)) for k in range(1, n_l)
     ]
+    g_copies = spread_rows(0, l)
     m_copies = [send(mg.at[p], mg.at[p], m_sem, (k - 1,), at(dp=k)) for k in range(1, n_p)]
     dec_copies = []
     for j, (start, width) in enumerate(dec_parts):
@@ -105,22 +129,12 @@
             dec_hbm.at[pl.ds(base, half), pl.ds(start, width)],
             wdec.at[:, pl.ds(start, width)], wdec_sem.at[j],
         )
-        copy.start()
+        copy.start(priority=1)
         dec_copies.append(copy)
-    for copy in copies:
+    for k, copy in enumerate(z_copies, 1):
         copy.wait_recv()
-    y_copies = [send(xg.at[t, p], xg.at[t, p], gy_sem, (k - 1,), at(dp=k)) for k in range(1, n_p)]
-    x_copies = [
-        send(xg.at[t, p], xg.at[t, p], gx_sem, (0, k - 1), at(dt=k)) for k in range(1, n_t)
-    ]
-    for m, copy in enumerate(y_copies, 1):
-        copy.wait_recv()
-        came = lax.rem(p + n_p - m, n_p)
-        x_copies += [
-            send(xg.at[t, came], xg.at[t, came], gx_sem, (m, k - 1), at(dt=k))
-            for k in range(1, n_t)
-        ]
-    for copy in x_copies:
+        g_copies += spread_rows(k, lax.rem(l + n_l - k, n_l))
+    for copy in g_copies:
         copy.wait_recv()
     block = 0
     for a in range(n_t):
@@ -141,10 +155,9 @@
         start, width = enc_parts[j]
         cols = pl.ds(start, width)
         e_copies[j].wait_recv()
-        bias = enc_bias[:, pl.ds(pl.multiple_of(base + start, 128), width)]
-        acts[:, cols] = jnp.maximum(pe[:, cols] + pr[:, cols] + bias, 0.0).astype(BF16)
-
-    a_copies, b_copies, c_copies = {}, {}, {}
+        acts[:, cols] = jnp.maximum(pe[:, cols] + pr[:, cols] + enc_bias[:, cols], 0.0).astype(BF16)
+
+    a_copies, c_copies = {}, {}
 
     def decode(c):
         start, width = dec_parts[c]
@@ -160,44 +173,24 @@
                 y = term if y is None else y + term
         else:
             y = jnp.dot(acts[...], wdec[:, cols], preferred_element_type=F32)
-        tall = total_rows // n_t
-        for a in range(n_t):
+        tall = n_l * rows
+        for a in range(n_t * n_p):
             piece = y[a * tall:(a + 1) * tall]
             ysend[a, :, cols] = piece.astype(BF16)
             yown[a, :, cols] = piece
         a_copies[c] = []
-        for k in range(1, n_t):
-            peer = at(dt=k)
-            a_copies[c].append(
-                send(ysend.at[peer[2], :, cols], yrecv.at[k - 1, :, cols], a_sem, (c, k - 1), peer)
-            )
-
-    def sum_x(c):
+        for k, (a, b) in enumerate(others):
+            peer = at(dp=a, dt=b)
+            theirs = ysend.at[peer[2] * n_p + peer[0], :, cols]
+            a_copies[c].append(send(theirs, yrecv.at[k, :, cols], a_sem, (c, k), peer))
+
+    def sum_xy(c):
         start, width = dec_parts[c]
         cols = pl.ds(start, width)
-        total = yown[t, :, cols]
+        total = yown[t * n_p + p, :, cols]
         for k, copy in enumerate(a_copies[c]):
             copy.wait_recv()
             total += yrecv[k, :, cols].astype(F32)
-        tall = total_rows // (n_t * n_p)
-        for a in range(n_p):
-            piece = total[a * tall:(a + 1) * tall]
-            bsend[a, :, cols] = piece.astype(BF16)
-            bown[a, :, cols] = piece
-        b_copies[c] = []
-        for k in range(1, n_p):
-            peer = at(dp=k)
-            b_copies[c].append(
-                send(bsend.at[peer[0], :, cols], brecv.at[k - 1, :, cols], b_sem, (c, k - 1), peer)
-            )
-
-    def sum_y(c):
-        start, width = dec_parts[c]
-        cols = pl.ds(start, width)
-        total = bown[p, :, cols]
-        for k, copy in enumerate(b_copies[c]):
-            copy.wait_recv()
-            total += brecv[k, :, cols].astype(F32)
         for a in range(n_l):
             piece = total[a * rows:(a + 1) * rows]
             csend[a, :, cols] = piece.astype(BF16)
@@ -225,40 +218,42 @@
         counts = jnp.maximum(jnp.sum(spread, axis=1, keepdims=True), 1.0)
         pooled = jnp.dot(spread.astype(BF16), acts[...], preferred_element_type=F32) / counts
         for a in range(n_p * n_t):
-            psend[a] = pooled[a * PAD:a * PAD + CAP].astype(BF16)
+            psend[a] = pooled[a * PAD:(a + 1) * PAD].astype(BF16)
         mine = p * n_t + t
         precv[mine] = psend[mine]
         copies = []
-        for a in range(n_p):
-            for b in range(n_t):
-                if a or b:
-                    peer = at(dp=a, dt=b)
-                    copies.append(
-                        send(psend.at[peer[0] * n_t + peer[2]], precv.at[mine], p_sem, (a, b), peer)
-                    )
+        for a, b in others:
+            peer = at(dp=a, dt=b)
+            theirs = psend.at[peer[0] * n_t + peer[2]]
+            copies.append(send(theirs, precv.at[mine], p_sem, (a, b), peer))
         return copies
 
     steps = len(dec_parts)
-    pool_copies = []
-    for c in range(steps + 3):
-        if c < steps:
-            decode(c)
-        if c == 0:
+    pool_copies, out_copies = [], []
+    for c in range(steps):
+        decode(c)
+        if c == steps - 1:
             pool_copies = pool()
-        if 0 <= c - 1 < steps:
-            sum_x(c - 1)
-        if 0 <= c - 2 < steps:
-            sum_y(c - 2)
-        if c == steps:
-            for copy in pool_copies:
-                copy.wait_recv()
-            for a in range(n_p):
-                for b in range(n_t):
-                    owned[:, pl.ds((b * n_p + a) * half, half)] = precv[a * n_t + b]
-        if 0 <= c - 3 < steps:
-            sum_z(c - 3)
+    for c in range(steps):
+        sum_xy(c)
+    for copy in pool_copies:
+        copy.wait_recv()
+    for a in range(n_p):
+        for b in range(n_t):
+            out_copies.append(pltpu.make_async_copy(
+                precv.at[a * n_t + b],
+                owned_hbm.at[:, pl.ds((b * n_p + a) * half, half)],
+                out_sem.at[1 + a * n_t + b],
+            ))
+            out_copies[-1].start()
+    for c in range(steps):
+        sum_z(c)
+    out_copies.append(pltpu.make_async_copy(recon, recon_hbm, out_sem.at[0]))
+    out_copies[-1].start()
     for copy in sent:
         copy.wait_send()
+    for copy in out_copies:
+        copy.wait()
 
 
 def per_device(sizes, resid, enc_weight, enc_bias, dec_weight, dec_bias, spans, owners):
@@ -268,21 +263,28 @@
     total = rows * n_p * n_l * n_t
     enc_parts = chunked(half, 1024)
     dec_parts = chunked(width, 512)
-    vmem = pl.BlockSpec(memory_space=pltpu.VMEM)
     hbm = pl.BlockSpec(memory_space=pl.ANY)
     dma = pltpu.SemaphoreType.DMA
-    x_rows, y_rows = total // n_t, total // (n_t * n_p)
+    planes, tall = n_t * n_p, n_l * rows
     more = lambda n: max(n - 1, 1)
     steps = len(dec_parts)
-    return pl.pallas_call(
+    out_shape = (
+        jax.ShapeDtypeStruct((rows, width), BF16),
+        jax.ShapeDtypeStruct((PAD, half * n_p * n_t), BF16),
+    )
+    recon, owned = pl.pallas_call(
         functools.partial(kernel, sizes, enc_parts, dec_parts),
-        out_shape=(
-            jax.ShapeDtypeStruct((rows, width), BF16),
-            jax.ShapeDtypeStruct((CAP, half * n_p * n_t), BF16),
-        ),
-        in_specs=[vmem, hbm, vmem, hbm, vmem, vmem, vmem],
-        out_specs=(vmem, vmem),
+        out_shape=out_shape,
+        in_specs=[hbm] * 7,
+        out_specs=(hbm, hbm),
         scratch_shapes=[
+            pltpu.VMEM((rows, width), BF16),
+            pltpu.VMEM((1, half), F32),
+            pltpu.VMEM((width,), F32),
+            pltpu.VMEM((1, width), F32),
+            pltpu.VMEM(spans.shape, jnp.int32),
+            pltpu.VMEM((1, owners.shape[0]), jnp.int32),
+            pltpu.VMEM((rows, width), BF16),
             pltpu.VMEM((width, half), BF16),
             pltpu.VMEM((half, width), BF16),
             pltpu.VMEM((n_t, n_p, n_l, rows, width), BF16),
@@ -292,26 +294,23 @@
             pltpu.VMEM((total, half), F32),
             pltpu.VMEM((total, half), F32),
             pltpu.VMEM((total, half), BF16),
-            pltpu.VMEM((n_t, x_rows, width), BF16),
-            pltpu.VMEM((n_t, x_rows, width), F32),
-            pltpu.VMEM((more(n_t), x_rows, width), BF16),
-            pltpu.VMEM((n_p, y_rows, width), BF16),
-            pltpu.VMEM((n_p, y_rows, width), F32),
-            pltpu.VMEM((more(n_p), y_rows, width), BF16),
+            pltpu.VMEM((planes, tall, width), BF16),
+            pltpu.VMEM((planes, tall, width), F32),
+            pltpu.VMEM((more(planes), tall, width), BF16),
             pltpu.VMEM((n_l, rows, width), BF16),
             pltpu.VMEM((n_l, rows, width), F32),
             pltpu.VMEM((more(n_l), rows, width), BF16),
-            pltpu.VMEM((n_p * n_t, CAP, half), BF16),
-            pltpu.VMEM((n_p * n_t, CAP, half), BF16),
+            pltpu.VMEM((n_p * n_t, PAD, half), BF16),
+            pltpu.VMEM((n_p * n_t, PAD, half), BF16),
+            dma((5,)),
+            dma((1 + planes,)),
             dma((len(enc_parts),)),
             dma((steps,)),
             dma((2, more(n_l))),
-            dma((2, more(n_p))),
-            dma((2, n_p, more(n_t))),
+            dma((2, n_l, n_p, n_t)),
             dma((2, more(n_p))),
             dma((2, len(enc_parts))),
-            dma((2, steps, more(n_t))),
-            dma((2, steps, more(n_p))),
+            dma((2, steps, more(planes))),
             dma((2, steps, more(n_l))),
             dma((2, n_p, n_t)),
         ],
@@ -322,8 +321,9 @@
             flops=4 * total * width * half, bytes_accessed=4 * width * half, transcendentals=0
         ),
     )(
-        resid, enc_weight, enc_bias[None, :], dec_weight, dec_bias[None, :], spans, owners[None, :]
-    )
+        resid, enc_weight, enc_bias[None, :], dec_weight, dec_bias, spans, owners[None, :]
+    )
+    return recon, owned[:CAP]
 
 
 def solution(mesh):

time: 44.5 us -> 31.7 us (0.71)
  Pallas kernels: 39.3 us -> 27.8 us
  local copies, waits for them, and re-layouts: 4.28 us -> 2.99 us
    pallas_call x1, Pallas kernels: 39.3 us -> 27.8 us  [per_device(): pl.pallas_call(functools.partial(kernel, sizes, enc_parts, dec_parts), ou...]
    broadcast_in_dim x1 -> x0, local copies, waits for them, and re-layouts: 1.3 us -> none  [per_device(): dec_bias[None, :]]
where the time goes in v2:
time: 31.7 us; the launch traced here: 31.4 us
  Pallas kernels  27.8 us (88%)
  local copies, waits for them, and re-layouts  2.99 us (9%)
  between operations  0.64 us (2%)
    pallas_call x1, Pallas kernels, per_device(): pl.pallas_call(functools.partial(kernel, sizes, enc_parts, dec_parts), ou...  27.8 us
    unnamed x2, local copies, waits for them, and re-layouts  2.99 us

profile of v2, /device:TPU:0, one launch (start us, length us, event | category | flops | bytes accessed | tf_op | source)
XLA Modules:
  0.0 31.4 jit_solution(4343984136134256482)
XLA Ops:
  0.6 27.8 %shard_map.86 = (bf16[4,1792]{1,0:T(4,128)(2,1)}, bf16[8,16384]{1,0:T(8,128)(2,1)}) custom-call(bf16[4,1792]{1,0:T(4,128)(2,1)} %resid_hbm.1, bf16[1792,8192]{1,0:T(8,128)(2,1)} %enc_hbm.1, f32[1,8192]{1,0:T(1,128)} %bitcast.4, bf16[8192,1792]{1,0:T(8,128)(2,1)} %dec_hbm.1, f32[1792]{0:T(1024)} %dec_bias_hbm.1, s32[8,32]{1,0:T(8,128)} %spans_hbm.1, ...), custom_call_target="tpu_custom_call" | custom-call | flops 1879048192 | bytes 29360128 | tf_op jit(solution)/shard_map/pallas_call | solution.py:275
  28.4 1.3 %copy.11 = bf16[4,1792]{1,0:T(4,128)(2,1)} copy(bf16[4,1792]{1,0:T(4,128)(2,1)} %get-tuple-element.8) | data formatting | bytes 28672
  29.8 1.7 %copy.12 = bf16[6,16384]{1,0:T(8,128)(2,1)} copy(bf16[6,16384]{1,0:T(8,128)(2,1)} %bitcast.3) | data formatting | bytes 393216
